TPU v7x, 32 devices: a whole 2x2x4 slice. The times are simulated.
32 devices in a mesh: row: 4 (over x, core), col: 8 (over z, y).
Axes of the slice: x: 2, y: 2, z: 4, core: 2. Of those that a mesh axis runs over, the one named last changes fastest.
Arguments:
- hidden: bfloat16 [512, 3584], P(('row', 'col')), may hold values from -6 to 6
- route_ids: int32 [512, 8], P(('row', 'col')), may hold values from 0 to 31, all different within a row; in each aligned block of 16 rows (0 to 15, 16 to 31, ...) at most 8 rows name the same one
- route_scores: float32 [512, 8], P(('row', 'col')), may hold values from 0.05 to 1
- gate_weight: bfloat16 [32, 3584, 1024], P(('row', 'col')), may hold values from -0.09375 to 0.09375
- up_weight: bfloat16 [32, 3584, 1024], P(('row', 'col')), may hold values from -0.09375 to 0.09375
- down_weight: bfloat16 [32, 1024, 3584], P(('row', 'col')), may hold values from -0.1875 to 0.1875
- queries: bfloat16 [512, 64, 576], P(('row', 'col'))
- latent_cache: bfloat16 [512, 128, 576], P(('row', 'col'))
- lengths: int32 [512], P(('row', 'col')), may hold values from 1 to 128, 32768 in all
Outputs:
- expert_mix: bfloat16 [512, 3584], P(('row', 'col'))
- context: bfloat16 [512, 64, 512], P(('row', 'col'))
Inputs may be any that keep to these rules, and one draw needn't show every extreme that they name: `route_ids`: among the 16 sequences of one device (aligned blocks of rows), no expert is named more than 8 times, and in every draw some expert is named exactly 8 times; each row names 8 different experts. `lengths`: some sequence fills all 128 slots.
All inputs are finite; a program needn't handle non-finite values. No bound on the sum of `lengths` on one device may be relied on, other than what follows from the above.
Results may differ from a plain program's by a relative error of at most 0.013.
Values may be sent and summed in bfloat16 or wider, within the bound.
A program may use at most 128 MiB of HBM per device.

v0:
```python
import functools

import jax
import jax.numpy as jnp
from jax import lax
from jax.experimental import pallas as pl
from jax.experimental.pallas import tpu as pltpu
from jax.sharding import PartitionSpec as P

MESH = pl.DeviceIdType.MESH
LATENT = 512
SCALE = 192 ** (-0.5)
DEPTH = 4
CHUNK = 512
HOP, BLOCK, WORK, FILL, FILL_FROM = 1.0, 0.42, 0.9, 1.5, 2.0


def bits_of(rows, cols):
    tall = cols // DEPTH
    bits = {"z": [], "y": [], "x": []}
    for axis, size, mesh_axis, stride in (("z", DEPTH, "col", tall), ("y", tall, "col", 1), ("x", rows // 2, "row", 2)):
        step = size // 2
        while step >= 1:
            bits[axis].append((axis, mesh_axis, stride * step, step))
            step //= 2
    return bits["z"] + bits["y"] + bits["x"] + [("core", "row", 1, 1 / 6)]


def runs_of(slots):
    runs = []
    for slot in sorted(slots):
        if runs and runs[-1][0] + runs[-1][1] == slot:
            runs[-1][1] += 1
        else:
            runs.append([slot, 1])
    return [tuple(run) for run in runs]


def held_before(order, stage):
    slots = [0]
    for bit in order[:stage]:
        slots += [slot | (1 << bit) for slot in slots]
    return sorted(slots)


def schedule(bits, orders, widths, backward, fillers):
    stages = len(bits)
    clock, free, out = 0.0, {}, []
    hops = [] if backward else [(0.0, chunk, 0) for chunk in range(len(orders))]
    if not backward:
        hops[-1] = (-1.0, len(orders) - 1, 0)
    work = list(range(len(orders))) if backward else []
    fill = list(range(fillers))
    table = backward
    while hops or work or fill:
        hops.sort()
        due = hops[0][0] if hops else float("inf")
        if due > clock + 0.2 and ((work and table) or (fill and clock > FILL_FROM)):
            if work and table:
                chunk = work.pop(0)
                out.append(("work", chunk, 0))
                clock += WORK
                if backward:
                    hops.append((clock, chunk, 0))
            else:
                out.append(("fill", fill.pop(0), 0))
                clock += FILL
            continue
        if not hops:
            clock += 0.5
            continue
        _, chunk, step = hops.pop(0)
        clock = max(clock, due) + 0.1
        out.append(("hop", chunk, step))
        if step > 0 and backward:
            clock += 0.02 * (1 << (stages - step))
        if step == stages:
            if widths[chunk] != CHUNK:
                table = True
                clock += 1.0
            elif not backward:
                work.append(chunk)
            continue
        stage = stages - 1 - step if backward else step
        link = orders[chunk][stage]
        axis, distance = bits[link][0], bits[link][3]
        start = max(clock, free.get(axis, 0.0))
        load = (1 << stage) * widths[chunk] / CHUNK * BLOCK
        end = start + load * distance
        free[axis] = start + load * min(distance, 1)
        hops.append((end + HOP, chunk, step + 1))
    return out, clock


def kernel(
    plan,
    ids_ref, scores_ref, len_ref, hidden_ref, wg_hbm, wu_hbm, wd_hbm, q_hbm, kv_hbm,
    mix_ref, ctx_hbm,
    xg, got, wg, wu, wd, qv, kv, ctx, pick, place, share, xc, gacc, uacc, units,
    gs_sem, gr_sem, ss_sem, sr_sem, w_sem, a_sem,
):
    bits, orders, ext, cap, rows, cols = plan
    stages, chunks = len(bits), len(orders) - 1
    seqs, width = hidden_ref.shape
    devices = rows * cols
    row, col = lax.axis_index("row"), lax.axis_index("col")
    me = row * cols + col

    def partner(bit):
        _, mesh_axis, stride, _ = bits[bit]
        own = row if mesh_axis == "row" else col
        other = own + stride * (1 - 2 * lax.rem(lax.div(own, stride), 2))
        return (other, col) if mesh_axis == "row" else (row, other)

    barrier = pltpu.get_barrier_semaphore()
    for bit in range(stages):
        pl.semaphore_signal(barrier, inc=1, device_id=partner(bit), device_id_type=MESH)

    loads = [
        pltpu.make_async_copy(q_hbm, qv, a_sem.at[0]),
        pltpu.make_async_copy(kv_hbm, kv, a_sem.at[1]),
    ]
    for load in loads:
        load.start()
    weight_loads = []
    for chunk in range(chunks):
        part = pl.ds(chunk * CHUNK, CHUNK)
        weight_loads.append((
            pltpu.make_async_copy(wg_hbm.at[0, part], wg.at[part], w_sem.at[0, chunk]),
            pltpu.make_async_copy(wu_hbm.at[0, part], wu.at[part], w_sem.at[1, chunk]),
        ))
    down_loads = [
        pltpu.make_async_copy(
            wd_hbm.at[0, :, pl.ds(chunk * CHUNK, CHUNK)], wd.at[:, pl.ds(chunk * CHUNK, CHUNK)], w_sem.at[2, chunk]
        )
        for chunk in range(chunks)
    ]

    scores = scores_ref[...]
    combine = 2.5 * scores / jnp.sum(scores, axis=0, keepdims=True)
    ids = ids_ref[...]
    square = (seqs, seqs)
    diagonal = lax.broadcasted_iota(jnp.int32, square, 0) == lax.broadcasted_iota(jnp.int32, square, 1)
    lane = lax.broadcasted_iota(jnp.int32, (seqs, ext), 1)
    table = jnp.zeros((seqs, ext), jnp.float32)
    for k in range(ids.shape[0]):
        weight = jnp.sum(jnp.where(diagonal, combine[k : k + 1], 0.0), axis=1, keepdims=True)
        expert = jnp.sum(jnp.where(diagonal, ids[k : k + 1].astype(jnp.float32), 0.0), axis=1, keepdims=True)
        expert = expert.astype(jnp.int32)
        high = weight.astype(jnp.bfloat16).astype(jnp.float32)
        table += jnp.where(lane == expert, high, 0.0) + jnp.where(lane == expert + devices, weight - high, 0.0)
    xg[0, :, pl.ds(0, ext)] = table.astype(jnp.bfloat16)
    xg[0, :, pl.ds(ext, width)] = hidden_ref[...]
    pl.semaphore_wait(barrier, stages)

    def columns(chunk):
        return pl.ds(0, ext) if chunk == chunks else pl.ds(ext + chunk * CHUNK, CHUNK)

    def gather_start(chunk, stage):
        bit = orders[chunk][stage]
        for first, count in runs_of(held_before(orders[chunk], stage)):
            pltpu.make_async_remote_copy(
                src_ref=xg.at[pl.ds(first, count), :, columns(chunk)],
                dst_ref=xg.at[pl.ds(first + (1 << bit), count), :, columns(chunk)],
                send_sem=gs_sem.at[chunk, stage], recv_sem=gr_sem.at[chunk, stage],
                device_id=partner(bit), device_id_type=MESH,
            ).start()

    def gather_wait(chunk, stage, sem):
        view = xg.at[pl.ds(0, 1 << stage), :, columns(chunk)]
        pltpu.make_async_copy(view, view, sem.at[chunk, stage]).wait()

    groups = devices // 16
    tokens = 16 * seqs
    slots = 16 * cap

    def routing():
        lane_of = lax.broadcasted_iota(jnp.int32, (16, ext), 1)
        row_of = lax.broadcasted_iota(jnp.int32, (16, ext), 0)
        chosen = jnp.where(lane_of == me + row_of * devices, 1.0, 0.0)
        chosen = jnp.where(row_of < 2, chosen, 0.0).astype(jnp.bfloat16)
        before = lax.broadcasted_iota(jnp.int32, (tokens, tokens), 0)
        after = lax.broadcasted_iota(jnp.int32, (tokens, tokens), 1)
        earlier = jnp.where((before // seqs == after // seqs) & (before < after), 1.0, 0.0).astype(jnp.bfloat16)
        slot = lax.broadcasted_iota(jnp.int32, (slots, tokens), 0)
        token = lax.broadcasted_iota(jnp.int32, (slots, tokens), 1)
        for group in range(groups):
            table = xg[pl.ds(16 * group, 16), :, pl.ds(0, ext)].reshape(tokens, ext)
            both = lax.dot_general(chosen, table, (((1,), (1,)), ((), ())), preferred_element_type=jnp.float32)
            named = jnp.where(both > 0.0, 1.0, 0.0)
            rank = jnp.dot(named.astype(jnp.bfloat16), earlier, preferred_element_type=jnp.float32)[0:1].astype(jnp.int32)
            weight = both[0:1] + both[1:2]
            hit = (slot // cap == token // seqs) & (rank == slot % cap) & (named[0:1] > 0.0)
            one = jnp.where(hit, 1.0, 0.0)
            share[pl.ds(group * slots, slots), :] = jnp.broadcast_to(
                jnp.sum(one * weight, axis=1, keepdims=True), (slots, 128)
            )
            pick[group] = one.astype(jnp.bfloat16)
            place[group] = one.T.astype(jnp.bfloat16)

    tile = 256
    total = groups * slots

    def up_chunk(chunk, first):
        here = pl.ds(ext + chunk * CHUNK, CHUNK)
        for group in range(groups):
            x = xg[pl.ds(16 * group, 16), :, here].reshape(tokens, CHUNK)
            xc[pl.ds(group * slots, slots), :] = jnp.dot(
                pick[group], x, preferred_element_type=jnp.float32
            ).astype(jnp.bfloat16)
        for load in weight_loads[chunk]:
            load.wait()

        def body(n, carry):
            at = pl.ds(pl.multiple_of(n * tile, tile), tile)
            for acc, w in ((gacc, wg), (uacc, wu)):
                part = jnp.dot(xc[...], w[pl.ds(chunk * CHUNK, CHUNK), at], preferred_element_type=jnp.float32)
                acc[:, at] = part if first else acc[:, at] + part
            return carry

        lax.fori_loop(0, gacc.shape[1] // tile, body, 0)

    def down_chunk(chunk):
        down_loads[chunk].wait()

        def body(n, carry):
            at = pl.ds(pl.multiple_of(chunk * CHUNK + n * tile, tile), tile)
            to = pl.ds(pl.multiple_of(ext + chunk * CHUNK + n * tile, 128), tile)
            out = jnp.dot(units[...], wd[:, at], preferred_element_type=jnp.float32)
            out = (out * share[:, 0:1]).astype(jnp.bfloat16)
            for group in range(groups):
                y = jnp.dot(place[group], out[group * slots : (group + 1) * slots], preferred_element_type=jnp.float32)
                xg[pl.ds(16 * group, 16), :, to] = y.astype(jnp.bfloat16).reshape(16, seqs, tile)
            return carry

        lax.fori_loop(0, CHUNK // tile, body, 0)

    group_of = min(4, seqs)

    def attend(first):
        own = range(first, first + group_of)
        scored = [jnp.dot(qv[i], kv[i], preferred_element_type=jnp.float32) * SCALE for i in own]
        slot = lax.broadcasted_iota(jnp.int32, scored[0].shape, 1)
        visible = [slot < len_ref[i] for i in own]
        scored = [jnp.where(seen, each, -1e30) for seen, each in zip(visible, scored)]
        top = [jnp.max(each, axis=-1, keepdims=True) for each in scored]
        numer = [jnp.where(seen, jnp.exp(each - most), 0.0) for seen, each, most in zip(visible, scored, top)]
        total = [jnp.sum(each, axis=-1, keepdims=True) for each in numer]
        prob = [(each / whole).astype(jnp.bfloat16) for each, whole in zip(numer, total)]
        for i, each in zip(own, prob):
            ctx[i] = lax.dot_general(
                each, kv[i, pl.ds(0, LATENT), :], (((1,), (1,)), ((), ())), preferred_element_type=jnp.float32
            ).astype(jnp.bfloat16)

    widths = [CHUNK] * chunks + [ext]
    steps, _ = schedule(bits, orders, widths, False, seqs // group_of)
    first_up = True
    for number, (kind, which, step) in enumerate(steps):
        if kind == "hop":
            if step > 0:
                gather_wait(which, step - 1, gr_sem)
            if step < stages:
                gather_start(which, step)
            elif which == chunks:
                routing()
        elif kind == "work":
            up_chunk(which, first_up)
            first_up = False
        else:
            if which == 0:
                for load in loads:
                    load.wait()
            attend(which * group_of)
        if number == chunks:
            for pair in weight_loads:
                for load in pair:
                    load.start()
            for load in down_loads:
                load.start()
    ctx_out = pltpu.make_async_copy(ctx, ctx_hbm, a_sem.at[2])
    ctx_out.start()

    def act(n, carry):
        at = pl.ds(pl.multiple_of(n * tile, tile), tile)
        gate = gacc[:, at]
        units[:, at] = (gate / (1.0 + jnp.exp(-gate)) * uacc[:, at]).astype(jnp.bfloat16)
        return carry

    lax.fori_loop(0, gacc.shape[1] // tile, act, 0)
    for chunk in range(chunks + 1):
        for stage in range(stages):
            gather_wait(chunk, stage, gs_sem)

    def scatter_start(chunk, stage):
        bit = orders[chunk][stage]
        at = 1 << stage
        for first, count in runs_of(held_before(orders[chunk], stage)):
            pltpu.make_async_remote_copy(
                src_ref=xg.at[pl.ds(first + (1 << bit), count), :, pl.ds(ext + chunk * CHUNK, CHUNK)],
                dst_ref=got.at[pl.ds(at, count), :, pl.ds(chunk * CHUNK, CHUNK)],
                send_sem=ss_sem.at[chunk, stage], recv_sem=sr_sem.at[chunk, stage],
                device_id=partner(bit), device_id_type=MESH,
            ).start()
            at += count

    def scatter_wait(chunk, stage, sem):
        view = got.at[pl.ds(1 << stage, 1 << stage), :, pl.ds(chunk * CHUNK, CHUNK)]
        pltpu.make_async_copy(view, view, sem.at[chunk, stage]).wait()

    def add(chunk, stage):
        at = 1 << stage
        here, there = pl.ds(ext + chunk * CHUNK, CHUNK), pl.ds(chunk * CHUNK, CHUNK)
        def one(slot, place):
            both = xg[slot, :, here].astype(jnp.float32) + got[place, :, there].astype(jnp.float32)
            xg[slot, :, here] = both.astype(jnp.bfloat16)

        for first, count in runs_of(held_before(orders[chunk], stage)):
            if count <= 4:
                for i in range(count):
                    one(first + i, at + i)
            else:

                def body(n, carry, first=first, at=at):
                    for i in range(4):
                        one(first + 4 * n + i, at + 4 * n + i)
                    return carry

                lax.fori_loop(0, count // 4, body, 0)
            at += count

    steps, _ = schedule(bits, orders[:chunks], [CHUNK] * chunks, True, 0)
    for kind, chunk, step in steps:
        if kind == "work":
            down_chunk(chunk)
            continue
        if step > 0:
            stage = stages - step
            scatter_wait(chunk, stage, sr_sem)
            if stage > 0:
                add(chunk, stage)
        if step < stages:
            scatter_start(chunk, stages - 1 - step)
        else:
            here, there = pl.ds(ext + chunk * CHUNK, CHUNK), pl.ds(chunk * CHUNK, CHUNK)
            both = xg[0, :, here].astype(jnp.float32) + got[1, :, there].astype(jnp.float32)
            mix_ref[:, there] = both.astype(jnp.bfloat16)
    for chunk in range(chunks):
        for stage in range(stages):
            scatter_wait(chunk, stage, ss_sem)
    ctx_out.wait()


def shards(rows, cols, hidden, route_ids, route_scores, gate_weight, up_weight, down_weight, queries, cache, lengths):
    seqs, width = hidden.shape
    hidden_units = gate_weight.shape[2]
    devices = rows * cols
    cap = max(2, 2 * seqs * route_ids.shape[1] // devices)
    ext = -(-2 * devices // 128) * 128
    bits = bits_of(rows, cols)
    stages = len(bits)
    z = [i for i, bit in enumerate(bits) if bit[0] == "z"]
    y = [i for i, bit in enumerate(bits) if bit[0] == "y"]
    x = [i for i, bit in enumerate(bits) if bit[0] == "x"]
    core = [stages - 1]
    chunks = width // CHUNK
    orders = [z + x + y, y + x + z, z + y + x, z + x + y, x + y + z, z + y + x, z + x + y]
    orders = [orders[i % len(orders)] + core for i in range(chunks)] + [z + y + x + core]
    groups = devices // 16
    slots = groups * 16 * cap
    sems = pltpu.SemaphoreType.DMA((chunks + 1, stages))
    vmem = pl.BlockSpec(memory_space=pltpu.VMEM)
    hbm = pl.BlockSpec(memory_space=pl.ANY)
    bf16, f32 = jnp.bfloat16, jnp.float32
    return pl.pallas_call(
        functools.partial(kernel, (bits, orders, ext, cap, rows, cols)),
        out_shape=(
            jax.ShapeDtypeStruct((seqs, width), bf16),
            jax.ShapeDtypeStruct(queries.shape[:2] + (LATENT,), bf16),
        ),
        in_specs=[vmem, vmem, pl.BlockSpec(memory_space=pltpu.SMEM), vmem, hbm, hbm, hbm, hbm, hbm],
        out_specs=(vmem, hbm),
        scratch_shapes=[
            pltpu.VMEM((devices, seqs, ext + width), bf16),
            pltpu.VMEM((devices, seqs, width), bf16),
            pltpu.VMEM(gate_weight.shape[1:], bf16),
            pltpu.VMEM(up_weight.shape[1:], bf16),
            pltpu.VMEM(down_weight.shape[1:], bf16),
            pltpu.VMEM(queries.shape, bf16),
            pltpu.VMEM(cache.shape[:1] + cache.shape[:0:-1], bf16),
            pltpu.VMEM(queries.shape[:2] + (LATENT,), bf16),
            pltpu.VMEM((groups, 16 * cap, 16 * seqs), bf16),
            pltpu.VMEM((groups, 16 * seqs, 16 * cap), bf16),
            pltpu.VMEM((slots, 128), f32),
            pltpu.VMEM((slots, CHUNK), bf16),
            pltpu.VMEM((slots, hidden_units), f32),
            pltpu.VMEM((slots, hidden_units), f32),
            pltpu.VMEM((slots, hidden_units), bf16),
            sems, sems, sems, sems,
            pltpu.SemaphoreType.DMA((3, chunks)),
            pltpu.SemaphoreType.DMA((3,)),
        ],
        compiler_params=pltpu.CompilerParams(
            collective_id=0, has_side_effects=True, vmem_limit_bytes=62 * 1024 * 1024
        ),
    )(
        route_ids.T, route_scores.T, lengths, hidden, gate_weight, up_weight, down_weight, queries, jnp.swapaxes(cache, 1, 2)
    )


def solution(mesh):
    both = ("row", "col")
    flat, deep = P(both, None), P(both, None, None)
    return jax.shard_map(
        functools.partial(shards, mesh.shape["row"], mesh.shape["col"]),
        mesh=mesh,
        in_specs=(flat, flat, flat, deep, deep, deep, deep, deep, P(both)),
        out_specs=(flat, deep),
        check_vma=False,
    )
```

profile of v0, /device:TPU:0, one launch (start us, length us, event | category | flops | bytes accessed | tf_op | source)
XLA Modules:
  0.0 69.5 jit_solution(16620744403525711254)
XLA Ops:
  0.6 65.0 %shard_map.104 = (bf16[16,3584]{1,0:T(8,128)(2,1)}, bf16[16,64,512]{2,1,0:T(8,128)(2,1)}) custom-call(s32[8,16]{1,0:T(8,128)} %bitcast.4, f32[8,16]{1,0:T(8,128)} %bitcast.5, s32[16]{0:T(128)} %len_ref.1, bf16[16,3584]{1,0:T(8,128)(2,1)} %hidden_ref.1, bf16[1,3584,1024]{2,1,0:T(8,128)(2,1)} %wg_hbm.1, bf16[1,3584,1024]{2,1,0:T(8,128)(2,1)} %wu_hbm.1, ...), custom_call_target="tpu_custom_call" | custom-call | tf_op jit(solution)/shard_map/pallas_call | solution.py:374
  65.7 1.6 %copy.13 = bf16[16,3584]{1,0:T(8,128)(2,1)} copy(bf16[16,3584]{1,0:T(8,128)(2,1)} %get-tuple-element.4) | data formatting | bytes 229376
  67.2 2.3 %copy.14 = bf16[16,64,512]{2,1,0:T(8,128)(2,1)} copy(bf16[16,64,512]{2,1,0:T(8,128)(2,1)} %get-tuple-element.5) | data formatting | bytes 2097152
where the time goes:
time: 69.7 us; the launch traced here: 69.5 us
  Pallas kernels  65 us (93%)
  local copies, waits for them, and re-layouts  3.84 us (6%)
    pallas_call x1, Pallas kernels, shards(): pl.pallas_call(functools.partial(kernel, (bits, orders, ext, cap, rows, c...  65 us
    unnamed x2, local copies, waits for them, and re-layouts  3.84 us

commit v1 on v0

--- a/solution.py
+++ b/solution.py
@@ -157,14 +157,18 @@
         return pl.ds(0, ext) if chunk == chunks else pl.ds(ext + chunk * CHUNK, CHUNK)
 
     def gather_start(chunk, stage):
-        bit = orders[chunk][stage]
-        for first, count in runs_of(held_before(orders[chunk], stage)):
-            pltpu.make_async_remote_copy(
-                src_ref=xg.at[pl.ds(first, count), :, columns(chunk)],
-                dst_ref=xg.at[pl.ds(first + (1 << bit), count), :, columns(chunk)],
-                send_sem=gs_sem.at[chunk, stage], recv_sem=gr_sem.at[chunk, stage],
-                device_id=partner(bit), device_id_type=MESH,
-            ).start()
+        order = orders[chunk]
+        held = held_before(order, stage)
+        fresh = sorted(set(held) - set(held_before(order, stage - 1))) if stage else held
+        hops = [(stage, held)] if stage < stages - 1 else []
+        for to, sent in hops + [(stages - 1, fresh)]:
+            for first, count in runs_of(sent):
+                pltpu.make_async_remote_copy(
+                    src_ref=xg.at[pl.ds(first, count), :, columns(chunk)],
+                    dst_ref=xg.at[pl.ds(first + (1 << order[to]), count), :, columns(chunk)],
+                    send_sem=gs_sem.at[chunk, to], recv_sem=gr_sem.at[chunk, to],
+                    device_id=partner(order[to]), device_id_type=MESH,
+                ).start()
 
     def gather_wait(chunk, stage, sem):
         view = xg.at[pl.ds(0, 1 << stage), :, columns(chunk)]
@@ -179,18 +183,19 @@
         row_of = lax.broadcasted_iota(jnp.int32, (16, ext), 0)
         chosen = jnp.where(lane_of == me + row_of * devices, 1.0, 0.0)
         chosen = jnp.where(row_of < 2, chosen, 0.0).astype(jnp.bfloat16)
-        before = lax.broadcasted_iota(jnp.int32, (tokens, tokens), 0)
-        after = lax.broadcasted_iota(jnp.int32, (tokens, tokens), 1)
-        earlier = jnp.where((before // seqs == after // seqs) & (before < after), 1.0, 0.0).astype(jnp.bfloat16)
-        slot = lax.broadcasted_iota(jnp.int32, (slots, tokens), 0)
-        token = lax.broadcasted_iota(jnp.int32, (slots, tokens), 1)
+        column = lax.broadcasted_iota(jnp.int32, (tokens, 1), 0)
+        token = lax.broadcasted_iota(jnp.int32, (1, tokens), 1)
+        slot = lax.broadcasted_iota(jnp.int32, (slots, 1), 0)
+        owner, slot_owner = token // seqs, slot // cap
+        slot_rank = slot - slot_owner * cap
+        earlier = jnp.where((column // seqs == owner) & (column < token), 1.0, 0.0).astype(jnp.bfloat16)
         for group in range(groups):
             table = xg[pl.ds(16 * group, 16), :, pl.ds(0, ext)].reshape(tokens, ext)
             both = lax.dot_general(chosen, table, (((1,), (1,)), ((), ())), preferred_element_type=jnp.float32)
             named = jnp.where(both > 0.0, 1.0, 0.0)
             rank = jnp.dot(named.astype(jnp.bfloat16), earlier, preferred_element_type=jnp.float32)[0:1].astype(jnp.int32)
             weight = both[0:1] + both[1:2]
-            hit = (slot // cap == token // seqs) & (rank == slot % cap) & (named[0:1] > 0.0)
+            hit = (slot_owner == owner) & (slot_rank == rank) & (named[0:1] > 0.0)
             one = jnp.where(hit, 1.0, 0.0)
             share[pl.ds(group * slots, slots), :] = jnp.broadcast_to(
                 jnp.sum(one * weight, axis=1, keepdims=True), (slots, 128)
@@ -291,30 +296,38 @@
         for stage in range(stages):
             gather_wait(chunk, stage, gs_sem)
 
+    def halves(chunk, stage):
+        held = held_before(orders[chunk], stage)
+        if stage < stages - 1:
+            return [(stage, 1 << stage, held)]
+        bit = 1 << orders[chunk][stage - 1]
+        near, far = [slot for slot in held if slot & bit], [slot for slot in held if not slot & bit]
+        return [(stage, 1 << stage, near), (stages, (1 << stage) + len(near), far)]
+
     def scatter_start(chunk, stage):
         bit = orders[chunk][stage]
-        at = 1 << stage
-        for first, count in runs_of(held_before(orders[chunk], stage)):
-            pltpu.make_async_remote_copy(
-                src_ref=xg.at[pl.ds(first + (1 << bit), count), :, pl.ds(ext + chunk * CHUNK, CHUNK)],
-                dst_ref=got.at[pl.ds(at, count), :, pl.ds(chunk * CHUNK, CHUNK)],
-                send_sem=ss_sem.at[chunk, stage], recv_sem=sr_sem.at[chunk, stage],
-                device_id=partner(bit), device_id_type=MESH,
-            ).start()
-            at += count
-
-    def scatter_wait(chunk, stage, sem):
-        view = got.at[pl.ds(1 << stage, 1 << stage), :, pl.ds(chunk * CHUNK, CHUNK)]
-        pltpu.make_async_copy(view, view, sem.at[chunk, stage]).wait()
-
-    def add(chunk, stage):
-        at = 1 << stage
+        for sem, at, part in halves(chunk, stage):
+            for first, count in runs_of(part):
+                pltpu.make_async_remote_copy(
+                    src_ref=xg.at[pl.ds(first + (1 << bit), count), :, pl.ds(ext + chunk * CHUNK, CHUNK)],
+                    dst_ref=got.at[pl.ds(at, count), :, pl.ds(chunk * CHUNK, CHUNK)],
+                    send_sem=ss_sem.at[chunk, sem], recv_sem=sr_sem.at[chunk, sem],
+                    device_id=partner(bit), device_id_type=MESH,
+                ).start()
+                at += count
+
+    def scatter_wait(chunk, sem, at, count, sems):
+        view = got.at[pl.ds(at, count), :, pl.ds(chunk * CHUNK, CHUNK)]
+        pltpu.make_async_copy(view, view, sems.at[chunk, sem]).wait()
+
+    def add(chunk, at, part):
         here, there = pl.ds(ext + chunk * CHUNK, CHUNK), pl.ds(chunk * CHUNK, CHUNK)
+
         def one(slot, place):
             both = xg[slot, :, here].astype(jnp.float32) + got[place, :, there].astype(jnp.float32)
             xg[slot, :, here] = both.astype(jnp.bfloat16)
 
-        for first, count in runs_of(held_before(orders[chunk], stage)):
+        for first, count in runs_of(part):
             if count <= 4:
                 for i in range(count):
                     one(first + i, at + i)
@@ -333,20 +346,23 @@
         if kind == "work":
             down_chunk(chunk)
             continue
-        if step > 0:
-            stage = stages - step
-            scatter_wait(chunk, stage, sr_sem)
-            if stage > 0:
-                add(chunk, stage)
-        if step < stages:
-            scatter_start(chunk, stages - 1 - step)
-        else:
+        parts = halves(chunk, stages - step) if step > 0 else []
+        for number, (sem, at, part) in enumerate(parts):
+            scatter_wait(chunk, sem, at, len(part), sr_sem)
+            if step < stages:
+                add(chunk, at, part)
+            if number == 0 and step < stages:
+                scatter_start(chunk, stages - 1 - step)
+        if step == 0:
+            scatter_start(chunk, stages - 1)
+        if step == stages:
             here, there = pl.ds(ext + chunk * CHUNK, CHUNK), pl.ds(chunk * CHUNK, CHUNK)
             both = xg[0, :, here].astype(jnp.float32) + got[1, :, there].astype(jnp.float32)
             mix_ref[:, there] = both.astype(jnp.bfloat16)
     for chunk in range(chunks):
         for stage in range(stages):
-            scatter_wait(chunk, stage, ss_sem)
+            for sem, at, part in halves(chunk, stage):
+                scatter_wait(chunk, sem, at, len(part), ss_sem)
     ctx_out.wait()
 
 
@@ -367,7 +383,7 @@
     orders = [orders[i % len(orders)] + core for i in range(chunks)] + [z + y + x + core]
     groups = devices // 16
     slots = groups * 16 * cap
-    sems = pltpu.SemaphoreType.DMA((chunks + 1, stages))
+    sems = pltpu.SemaphoreType.DMA((chunks + 1, stages + 1))
     vmem = pl.BlockSpec(memory_space=pltpu.VMEM)
     hbm = pl.BlockSpec(memory_space=pl.ANY)
     bf16, f32 = jnp.bfloat16, jnp.float32

time: 69.7 us -> 69.6 us (level)
  no operation moved by 1% of the time
where the time goes in v1:
time: 69.6 us; the launch traced here: 69.3 us
  Pallas kernels  64.9 us (93%)
  local copies, waits for them, and re-layouts  3.84 us (6%)
    pallas_call x1, Pallas kernels, shards(): pl.pallas_call(functools.partial(kernel, (bits, orders, ext, cap, rows, c...  64.9 us
    unnamed x2, local copies, waits for them, and re-layouts  3.84 us

profile of v1, /device:TPU:0, one launch (start us, length us, event | category | flops | bytes accessed | tf_op | source)
XLA Modules:
  0.0 69.3 jit_solution(17565138172584053271)
XLA Ops:
  0.6 64.9 %shard_map.104 = (bf16[16,3584]{1,0:T(8,128)(2,1)}, bf16[16,64,512]{2,1,0:T(8,128)(2,1)}) custom-call(s32[8,16]{1,0:T(8,128)} %bitcast.4, f32[8,16]{1,0:T(8,128)} %bitcast.5, s32[16]{0:T(128)} %len_ref.1, bf16[16,3584]{1,0:T(8,128)(2,1)} %hidden_ref.1, bf16[1,3584,1024]{2,1,0:T(8,128)(2,1)} %wg_hbm.1, bf16[1,3584,1024]{2,1,0:T(8,128)(2,1)} %wu_hbm.1, ...), custom_call_target="tpu_custom_call" | custom-call | tf_op jit(solution)/shard_map/pallas_call | solution.py:390
  65.5 1.6 %copy.13 = bf16[16,3584]{1,0:T(8,128)(2,1)} copy(bf16[16,3584]{1,0:T(8,128)(2,1)} %get-tuple-element.4) | data formatting | bytes 229376
  67.1 2.3 %copy.14 = bf16[16,64,512]{2,1,0:T(8,128)(2,1)} copy(bf16[16,64,512]{2,1,0:T(8,128)(2,1)} %get-tuple-element.5) | data formatting | bytes 2097152

commit v2 on v1

--- a/solution.py
+++ b/solution.py
@@ -12,7 +12,7 @@
 SCALE = 192 ** (-0.5)
 DEPTH = 4
 CHUNK = 512
-HOP, BLOCK, WORK, FILL, FILL_FROM = 1.0, 0.42, 0.9, 1.5, 2.0
+HOP, BLOCK, WORK, FILL, FILL_FROM = 1.5, 0.36, 0.9, 1.5, 2.0
 
 
 def bits_of(rows, cols):
@@ -23,7 +23,7 @@
         while step >= 1:
             bits[axis].append((axis, mesh_axis, stride * step, step))
             step //= 2
-    return bits["z"] + bits["y"] + bits["x"] + [("core", "row", 1, 1 / 6)]
+    return bits["z"] + bits["y"] + bits["x"] + [("core", "row", 1, 1 / 4)]
 
 
 def runs_of(slots):
@@ -259,8 +259,14 @@
 
     widths = [CHUNK] * chunks + [ext]
     steps, _ = schedule(bits, orders, widths, False, seqs // group_of)
+    needed = [which for kind, which, _ in steps if kind == "work"]
+    pending = [weight_loads[which] for which in needed] + [(load,) for load in down_loads]
+    before_work = [kind == "work" for kind, _, _ in steps].index(True)
+    early = sum(kind == "hop" for kind, _, _ in steps[:before_work]) - chunks - 1
+    spread = max(1, early // chunks)
+    hops = 0
     first_up = True
-    for number, (kind, which, step) in enumerate(steps):
+    for kind, which, step in steps:
         if kind == "hop":
             if step > 0:
                 gather_wait(which, step - 1, gr_sem)
@@ -269,6 +275,9 @@
             elif which == chunks:
                 routing()
         elif kind == "work":
+            while len(pending) >= 2 * chunks - needed.index(which):
+                for load in pending.pop(0):
+                    load.start()
             up_chunk(which, first_up)
             first_up = False
         else:
@@ -276,12 +285,14 @@
                 for load in loads:
                     load.wait()
             attend(which * group_of)
-        if number == chunks:
-            for pair in weight_loads:
-                for load in pair:
+        if kind == "hop":
+            hops += 1
+            if hops > chunks + 1 and pending and (hops - chunks) % spread == 0:
+                for load in pending.pop(0):
                     load.start()
-            for load in down_loads:
-                load.start()
+    for rest in pending:
+        for load in rest:
+            load.start()
     ctx_out = pltpu.make_async_copy(ctx, ctx_hbm, a_sem.at[2])
     ctx_out.start()
 

time: 69.6 us -> 72 us (1.034)
  Pallas kernels: 64.9 us -> 67.3 us
    pallas_call x1, Pallas kernels: 64.9 us -> 67.3 us  [shards(): pl.pallas_call(functools.partial(kernel, (bits, orders, ext, cap, rows, c...]
where the time goes in v2:
time: 72 us; the launch traced here: 71.8 us
  Pallas kernels  67.3 us (93%)
  local copies, waits for them, and re-layouts  3.84 us (5%)
    pallas_call x1, Pallas kernels, shards(): pl.pallas_call(functools.partial(kernel, (bits, orders, ext, cap, rows, c...  67.3 us
    unnamed x2, local copies, waits for them, and re-layouts  3.84 us

profile of v2, /device:TPU:0, one launch (start us, length us, event | category | flops | bytes accessed | tf_op | source)
XLA Modules:
  0.0 71.8 jit_solution(12898386832346440179)
XLA Ops:
  0.6 67.3 %shard_map.104 = (bf16[16,3584]{1,0:T(8,128)(2,1)}, bf16[16,64,512]{2,1,0:T(8,128)(2,1)}) custom-call(s32[8,16]{1,0:T(8,128)} %bitcast.4, f32[8,16]{1,0:T(8,128)} %bitcast.5, s32[16]{0:T(128)} %len_ref.1, bf16[16,3584]{1,0:T(8,128)(2,1)} %hidden_ref.1, bf16[1,3584,1024]{2,1,0:T(8,128)(2,1)} %wg_hbm.1, bf16[1,3584,1024]{2,1,0:T(8,128)(2,1)} %wu_hbm.1, ...), custom_call_target="tpu_custom_call" | custom-call | tf_op jit(solution)/shard_map/pallas_call | solution.py:401
  67.9 1.6 %copy.13 = bf16[16,3584]{1,0:T(8,128)(2,1)} copy(bf16[16,3584]{1,0:T(8,128)(2,1)} %get-tuple-element.4) | data formatting | bytes 229376
  69.5 2.3 %copy.14 = bf16[16,64,512]{2,1,0:T(8,128)(2,1)} copy(bf16[16,64,512]{2,1,0:T(8,128)(2,1)} %get-tuple-element.5) | data formatting | bytes 2097152

commit v3 on v1

--- a/solution.py
+++ b/solution.py
@@ -11,8 +11,8 @@
 LATENT = 512
 SCALE = 192 ** (-0.5)
 DEPTH = 4
-CHUNK = 512
-HOP, BLOCK, WORK, FILL, FILL_FROM = 1.0, 0.42, 0.9, 1.5, 2.0
+CHUNK = 896
+HOP, BLOCK, WORK, FILL, FILL_FROM = 1.0, 0.65, 1.5, 1.5, 2.0
 
 
 def bits_of(rows, cols):
@@ -228,17 +228,14 @@
     def down_chunk(chunk):
         down_loads[chunk].wait()
 
-        def body(n, carry):
-            at = pl.ds(pl.multiple_of(chunk * CHUNK + n * tile, tile), tile)
-            to = pl.ds(pl.multiple_of(ext + chunk * CHUNK + n * tile, 128), tile)
+        for start in range(0, CHUNK, tile):
+            wide = min(tile, CHUNK - start)
+            at, to = pl.ds(chunk * CHUNK + start, wide), pl.ds(ext + chunk * CHUNK + start, wide)
             out = jnp.dot(units[...], wd[:, at], preferred_element_type=jnp.float32)
             out = (out * share[:, 0:1]).astype(jnp.bfloat16)
             for group in range(groups):
                 y = jnp.dot(place[group], out[group * slots : (group + 1) * slots], preferred_element_type=jnp.float32)
-                xg[pl.ds(16 * group, 16), :, to] = y.astype(jnp.bfloat16).reshape(16, seqs, tile)
-            return carry
-
-        lax.fori_loop(0, CHUNK // tile, body, 0)
+                xg[pl.ds(16 * group, 16), :, to] = y.astype(jnp.bfloat16).reshape(16, seqs, wide)
 
     group_of = min(4, seqs)
 
@@ -379,7 +376,7 @@
     x = [i for i, bit in enumerate(bits) if bit[0] == "x"]
     core = [stages - 1]
     chunks = width // CHUNK
-    orders = [z + x + y, y + x + z, z + y + x, z + x + y, x + y + z, z + y + x, z + x + y]
+    orders = [z + x + y, y + x + z, z + y + x, z + x + y]
     orders = [orders[i % len(orders)] + core for i in range(chunks)] + [z + y + x + core]
     groups = devices // 16
     slots = groups * 16 * cap

time: 69.6 us -> 73.8 us (1.060)
  Pallas kernels: 64.9 us -> 69.1 us
    pallas_call x1, Pallas kernels: 64.9 us -> 69.1 us  [shards(): pl.pallas_call(functools.partial(kernel, (bits, orders, ext, cap, rows, c...]
where the time goes in v3:
time: 73.8 us; the launch traced here: 73.6 us
  Pallas kernels  69.1 us (94%)
  local copies, waits for them, and re-layouts  3.84 us (5%)
    pallas_call x1, Pallas kernels, shards(): pl.pallas_call(functools.partial(kernel, (bits, orders, ext, cap, rows, c...  69.1 us
    unnamed x2, local copies, waits for them, and re-layouts  3.84 us

profile of v3, /device:TPU:0, one launch (start us, length us, event | category | flops | bytes accessed | tf_op | source)
XLA Modules:
  0.0 73.6 jit_solution(145997477638984059)
XLA Ops:
  0.6 69.1 %shard_map.104 = (bf16[16,3584]{1,0:T(8,128)(2,1)}, bf16[16,64,512]{2,1,0:T(8,128)(2,1)}) custom-call(s32[8,16]{1,0:T(8,128)} %bitcast.4, f32[8,16]{1,0:T(8,128)} %bitcast.5, s32[16]{0:T(128)} %len_ref.1, bf16[16,3584]{1,0:T(8,128)(2,1)} %hidden_ref.1, bf16[1,3584,1024]{2,1,0:T(8,128)(2,1)} %wg_hbm.1, bf16[1,3584,1024]{2,1,0:T(8,128)(2,1)} %wu_hbm.1, ...), custom_call_target="tpu_custom_call" | custom-call | tf_op jit(solution)/shard_map/pallas_call | solution.py:387
  69.7 1.6 %copy.13 = bf16[16,3584]{1,0:T(8,128)(2,1)} copy(bf16[16,3584]{1,0:T(8,128)(2,1)} %get-tuple-element.4) | data formatting | bytes 229376
  71.3 2.3 %copy.14 = bf16[16,64,512]{2,1,0:T(8,128)(2,1)} copy(bf16[16,64,512]{2,1,0:T(8,128)(2,1)} %get-tuple-element.5) | data formatting | bytes 2097152
